TPU v7x, 32 devices: a whole 2x2x4 slice. The times are simulated.
32 devices in a mesh: ctx: 8 (over z, x), ch: 4 (over y, core).
Axes of the slice: x: 2, y: 2, z: 4, core: 2. Of those that a mesh axis runs over, the one named last changes fastest.
Arguments:
- inputs: float32 [4, 2048, 1024], P(None, 'ctx', 'ch'), may hold values from -6 to 6
- cotangent: float32 [4, 2048, 1024], P(None, 'ctx', 'ch'), may hold values from -6 to 6
- filters: float32 [2048, 1024], P('ctx', 'ch'), may hold values from -6 to 6
Outputs:
- input_grad: float32 [4, 2048, 1024], P(None, 'ctx', 'ch')
- filter_grad: float32 [2048, 1024], P('ctx', 'ch')
All inputs are finite; a program needn't handle non-finite values.
Results may differ from a plain program's by a relative error of at most 0.0001.
Values sent between devices are 32-bit elements; how exact they have to be, the bound alone decides.
A program may use at most 128 MiB of HBM per device.

v0:
```python
import math

import jax
import jax.numpy as jnp
from jax import lax
from jax.sharding import PartitionSpec as P

HIGHEST = lax.Precision.HIGHEST


def swapped(value, axis, apart):
    mask = 2**apart
    pairs = [(source, source ^ mask) for source in range(lax.axis_size(axis))]
    return lax.ppermute(value, axis, pairs)


def spin(outer, inner, period):
    turns = outer[:, None] * inner[None, :] % period
    angle = turns.astype(jnp.float32) * (2.0 * math.pi / period)
    return (jnp.cos(angle), jnp.sin(angle))


def times_complex(left, right):
    return jnp.stack(
        [left[0] * right[0] - left[1] * right[1], left[0] * right[1] + left[1] * right[0]]
    )


def conjugate(value):
    return jnp.stack([value[0], -value[1]])


def channel_mirror(value):
    flipped = value[..., ::-1]
    for bit in range(lax.axis_size("ch").bit_length() - 1):
        flipped = swapped(flipped, "ch", bit)
    return flipped


def forward_transform(stacked):
    count = lax.axis_size("ctx")
    width = stacked.shape[1]
    block = width // count
    period = count * width
    here = lax.axis_index("ctx")
    pieces = lax.all_to_all(stacked[:, None], "ctx", split_axis=2, concat_axis=1, tiled=True)
    across = jnp.arange(count, dtype=jnp.int32)
    cos_n, sin_n = spin(across, across, count)
    real_part = jnp.einsum("pi,kijc->kpjc", cos_n, pieces, precision=HIGHEST)
    imag_part = -jnp.einsum("pi,kijc->kpjc", sin_n, pieces, precision=HIGHEST)
    local = here * block + jnp.arange(block, dtype=jnp.int32)
    cos_t, sin_t = spin(across, local, period)
    cos_t = cos_t[:, :, None]
    sin_t = sin_t[:, :, None]
    turned = jnp.stack(
        [real_part * cos_t + imag_part * sin_t, imag_part * cos_t - real_part * sin_t]
    )
    rows = jnp.arange(width, dtype=jnp.int32)
    cos_m, sin_m = spin(rows, rows, width)
    gathered = lax.all_to_all(turned, "ctx", split_axis=2, concat_axis=3, tiled=True)
    real_in = gathered[0, :, 0]
    imag_in = gathered[1, :, 0]
    real_out = jnp.einsum("mj,kjc->kmc", cos_m, real_in, precision=HIGHEST) + jnp.einsum(
        "mj,kjc->kmc", sin_m, imag_in, precision=HIGHEST
    )
    imag_out = jnp.einsum("mj,kjc->kmc", cos_m, imag_in, precision=HIGHEST) - jnp.einsum(
        "mj,kjc->kmc", sin_m, real_in, precision=HIGHEST
    )
    return jnp.stack([real_out, imag_out])


def inverse_transform(spectra):
    count = lax.axis_size("ctx")
    width = spectra.shape[2]
    period = count * width
    here = lax.axis_index("ctx")
    rows = jnp.arange(width, dtype=jnp.int32)
    cos_m, sin_m = spin(rows, rows, width)
    real_in = spectra[0]
    imag_in = spectra[1]
    real_part = jnp.einsum("jm,kmc->kjc", cos_m, real_in, precision=HIGHEST) - jnp.einsum(
        "jm,kmc->kjc", sin_m, imag_in, precision=HIGHEST
    )
    imag_part = jnp.einsum("jm,kmc->kjc", sin_m, real_in, precision=HIGHEST) + jnp.einsum(
        "jm,kmc->kjc", cos_m, imag_in, precision=HIGHEST
    )
    turns = rows * here % period
    angle = turns.astype(jnp.float32) * (2.0 * math.pi / period)
    cos_t = jnp.cos(angle)[None, :, None]
    sin_t = jnp.sin(angle)[None, :, None]
    turned = jnp.stack(
        [real_part * cos_t - imag_part * sin_t, real_part * sin_t + imag_part * cos_t]
    )[:, :, None]
    across = jnp.arange(count, dtype=jnp.int32)
    cos_n, sin_n = spin(across, across, count)
    gathered = lax.all_to_all(turned, "ctx", split_axis=3, concat_axis=2, tiled=True)
    blocks = jnp.einsum("iq,kqjc->kijc", cos_n, gathered[0], precision=HIGHEST) - jnp.einsum(
        "iq,kqjc->kijc", sin_n, gathered[1], precision=HIGHEST
    )
    merged = lax.all_to_all(blocks, "ctx", split_axis=1, concat_axis=2, tiled=True)
    return merged[:, 0]


def body(inputs, cotangent, filters):
    seqs = inputs.shape[0]
    width = inputs.shape[1]
    period = lax.axis_size("ctx") * width
    factor = 1.0 / (period * math.sqrt(2.0 * period))
    stacked = jnp.concatenate([inputs, cotangent, filters[None]], axis=0)
    spectra = forward_transform(stacked)
    data_spec = spectra[:, :seqs]
    grad_spec = spectra[:, seqs : 2 * seqs]
    filt_spec = spectra[:, 2 * seqs :]
    filt_back = channel_mirror(filt_spec)
    effective = filt_spec + conjugate(filt_back)
    input_spec = times_complex(conjugate(effective), grad_spec)
    cross = jnp.sum(times_complex(grad_spec, conjugate(data_spec)), axis=1, keepdims=True)
    cross = cross + conjugate(channel_mirror(cross))
    combined = jnp.concatenate([input_spec, cross], axis=1)
    grads = inverse_transform(combined) * factor
    return (grads[:seqs], grads[seqs])


def solution(mesh):
    in_specs = (P(None, "ctx", "ch"), P(None, "ctx", "ch"), P("ctx", "ch"))
    out_specs = (P(None, "ctx", "ch"), P("ctx", "ch"))
    return jax.shard_map(body, mesh=mesh, in_specs=in_specs, out_specs=out_specs, check_vma=False)
```

profile of v0, /device:TPU:0, one launch (start us, length us, event | category | flops | bytes accessed | tf_op | source)
XLA Modules:
  0.0 361.8 jit_solution(14420741020888780935)
XLA Ops:
  0.6 1.8 maximum_bitcast_fusion.1
  2.4 3.9 %copy.63 = f32[9,1,256,256]{3,1,0,2:T(1,128)} copy(f32[9,1,256,256]{3,2,0,1:T(8,128)S(1)} %maximum_bitcast_fusion.1) | data formatting | bytes 4718592 | tf_op jit(solution)/shard_map/broadcast_in_dim | solution.py:46
  6.3 7.6 %all-to-all-start = ((f32[9,1,256,256]{3,1,0,2:T(1,128)}), f32[9,1,256,256]{3,1,0,2:T(1,128)S(1)}, u32[]{:S(2)}, u32[]{:S(2)}) async-start(f32[9,1,256,256]{3,1,0,2:T(1,128)} %copy.63), calls=%async_computation | async-start | bytes 4718592 | tf_op jit(solution)/shard_map/all_to_all | solution.py:46
  14.0 53.6 %all-to-all-done = f32[9,1,256,256]{3,1,0,2:T(1,128)S(1)} async-done(((f32[9,1,256,256]{3,1,0,2:T(1,128)}), f32[9,1,256,256]{3,1,0,2:T(1,128)S(1)}, u32[]{:S(2)}, u32[]{:S(2)}) %all-to-all-start) | async-done | bytes 2359328 | tf_op jit(solution)/shard_map/all_to_all | solution.py:46
  67.9 3.6 fusion.4
  71.5 4.1 %fusion.1 = (f32[1,9,8,32,256]{4,2,3,1,0:T(8,128)S(1)}, f32[1,9,8,32,256]{4,2,3,1,0:T(8,128)S(1)}) fusion(f32[9,32,256,8]{2,3,1,0:T(8,128)S(1)} %fusion.4, f32[8,32]{0,1:T(8,128)S(1)} %get-tuple-element.21, f32[8,32]{0,1:T(8,128)S(1)} %get-tuple-element.20, f32[9,8,32,256]{3,2,1,0:T(8,128)S(1)} %bitcast.116), kind=kOutput, calls=%fused_computation.7 | convolution fusion | flops 60752768 | bytes 9439232 | tf_op jit(solution)/shard_map/pi,kijc->kpjc/dot_general | solution.py:49
  76.0 1.5 copy.67
  77.5 108.0 %all_to_all.19 = f32[2,9,8,32,256]{4,3,1,0,2:T(8,128)S(1)} all-to-all(f32[2,9,8,32,256]{4,3,1,0,2:T(8,128)S(1)} %copy.67), channel_id=1, replica_groups=mesh['ctx'=8,'ch'=4] {'ctx'}, dimensions={2} | all-to-all | bytes 9437184 | tf_op jit(solution)/shard_map/all_to_all | solution.py:60
  186.5 4.9 %fusion.26 = f32[9,256,256]{2,1,0:T(8,128)S(1)} fusion(f32[9,256,256]{2,1,0:T(8,128)S(1)} %bitcast.111), kind=kOutput, calls=%fused_computation.60 | convolution fusion | flops 1812856832 | bytes 4718592 | tf_op jit(solution)/shard_map/mj,kjc->kmc/dot_general | solution.py:63
  191.7 4.9 %fusion.24 = f32[9,256,256]{2,1,0:T(8,128)S(1)} fusion(f32[9,256,256]{2,1,0:T(8,128)S(1)} %bitcast.113), kind=kOutput, calls=%fused_computation.58 | convolution fusion | flops 1812856832 | bytes 4718592 | tf_op jit(solution)/shard_map/mj,kjc->kmc/dot_general | solution.py:66
  196.6 5.1 %add_bitcast_fusion = f32[1,9,256,256]{2,3,1,0:T(8,128)S(1)} fusion(f32[9,256,256]{2,1,0:T(8,128)S(1)} %fusion.26, f32[9,256,256]{2,1,0:T(8,128)S(1)} %bitcast.114), kind=kOutput, calls=%fused_computation.13 | convolution fusion | flops 1813446656 | bytes 7077888 | tf_op jit(solution)/shard_map/mj,kjc->kmc/dot_general | solution.py:63
  201.7 4.9 %subtract_bitcast_fusion = f32[1,9,256,256]{2,3,1,0:T(8,128)S(1)} fusion(f32[9,256,256]{2,1,0:T(8,128)S(1)} %fusion.24, f32[9,256,256]{2,1,0:T(8,128)S(1)} %bitcast.112), kind=kOutput, calls=%fused_computation.12 | convolution fusion | flops 1813446656 | bytes 7077888 | tf_op jit(solution)/shard_map/mj,kjc->kmc/dot_general | solution.py:66
  206.6 1.4 copy-done
  208.5 1.9 collective-permute-done
  210.4 1.5 collective-permute-start.1
  211.9 12.4 %collective-permute-done.1 = f32[2,1,256,256]{2,3,1,0:T(8,128)S(1)} collective-permute-done((f32[2,1,256,256]{2,3,1,0:T(8,128)S(1)}, f32[2,1,256,256]{2,3,1,0:T(8,128)S(1)}, u32[]{:S(2)}, u32[]{:S(2)}) %collective-permute-start.1) | collective-permute-done | bytes 524320 | tf_op jit(solution)/shard_map/ppermute | solution.py:14
  224.5 1.5 multiply_subtract_fusion.1
  226.7 1.9 collective-permute-done.2
  228.6 1.5 collective-permute-start.3
  230.2 12.4 %collective-permute-done.3 = f32[2,1,256,256]{2,3,1,0:T(8,128)S(1)} collective-permute-done((f32[2,1,256,256]{2,3,1,0:T(8,128)S(1)}, f32[2,1,256,256]{2,3,1,0:T(8,128)S(1)}, u32[]{:S(2)}, u32[]{:S(2)}) %collective-permute-start.3) | collective-permute-done | bytes 524320 | tf_op jit(solution)/shard_map/ppermute | solution.py:14
  243.0 2.2 fusion.13
  245.2 2.2 fusion.12
  247.4 2.2 convolution_subtract_fusion
  249.6 2.5 subtract_bitcast_fusion.1
  252.4 3.2 copy.75
  255.6 63.1 %all_to_all.40 = f32[2,5,1,256,256]{4,0,2,1,3:T(2,128)S(1)} all-to-all(f32[2,5,1,256,256]{4,0,2,1,3:T(2,128)} %copy.75), channel_id=1, replica_groups=mesh['ctx'=8,'ch'=4] {'ctx'}, dimensions={3} | all-to-all | bytes 5242880 | tf_op jit(solution)/shard_map/all_to_all | solution.py:96
  318.8 2.0 fusion.119
  320.9 1.9 fusion.10
  323.0 2.0 fusion.8
  325.4 34.2 %all_to_all.41 = f32[5,8,32,256]{3,2,0,1:T(8,128)S(1)} all-to-all(f32[5,8,32,256]{3,2,0,1:T(8,128)S(1)} %copy.80), channel_id=1, replica_groups=mesh['ctx'=8,'ch'=4] {'ctx'}, dimensions={1} | all-to-all | bytes 2621440 | tf_op jit(solution)/shard_map/all_to_all | solution.py:100
  359.8 1.1 slice.119
  360.8 0.7 slice.120
  (30 shorter events, 4.8 us)
Async XLA Ops:
  6.3 61.4 %all-to-all-start = ((f32[9,1,256,256]{3,1,0,2:T(1,128)}), f32[9,1,256,256]{3,1,0,2:T(1,128)S(1)}, u32[]{:S(2)}, u32[]{:S(2)}) async-start(f32[9,1,256,256]{3,1,0,2:T(1,128)} %copy.63), calls=%async_computation | async-start | bytes 4718592 | tf_op jit(solution)/shard_map/all_to_all | solution.py:46
  206.6 1.4 copy-start
  208.4 16.1 %copy-start.1 = (f32[1,9,256,256]{2,3,1,0:T(8,128)S(1)}, f32[1,9,256,256]{2,3,1,0:T(8,128)}, u32[]{:S(2)}) copy-start(f32[1,9,256,256]{2,3,1,0:T(8,128)} %copy-done) | copy-start | bytes 7077892
  208.4 2.0 collective-permute-start
  210.4 14.0 %collective-permute-start.1 = (f32[2,1,256,256]{2,3,1,0:T(8,128)S(1)}, f32[2,1,256,256]{2,3,1,0:T(8,128)S(1)}, u32[]{:S(2)}, u32[]{:S(2)}) collective-permute-start(f32[2,1,256,256]{2,3,1,0:T(8,128)S(1)} %collective-permute-done), channel_id=1, source_target_pairs={{0,2},{1,3},{2,0},{3,1},{4,6},{5,7},{6,4},{7,5},{8,10},{9,11},{10,... | collective-permute-start | bytes 1572872 | tf_op jit(solution)/shard_map/ppermute | solution.py:14
  226.2 16.6 %copy-start.2 = (f32[1,4,256,256]{2,3,1,0:T(8,128)S(1)}, f32[1,4,256,256]{2,3,1,0:T(8,128)}, u32[]{:S(2)}) copy-start(f32[1,4,256,256]{2,3,1,0:T(8,128)} %get-tuple-element.3) | copy-start | bytes 3145732
  226.7 2.0 collective-permute-start.2
  228.6 14.0 %collective-permute-start.3 = (f32[2,1,256,256]{2,3,1,0:T(8,128)S(1)}, f32[2,1,256,256]{2,3,1,0:T(8,128)S(1)}, u32[]{:S(2)}, u32[]{:S(2)}) collective-permute-start(f32[2,1,256,256]{2,3,1,0:T(8,128)S(1)} %collective-permute-done.2), channel_id=1, source_target_pairs={{0,2},{1,3},{2,0},{3,1},{4,6},{5,7},{6,4},{7,5},{8,10},{9,11},{10,... | collective-permute-start | bytes 1572872 | tf_op jit(solution)/shard_map/ppermute | solution.py:14
where the time goes:
time: 365 us; the launch traced here: 362 us
  blocking collectives  205 us (56%)
  waiting for transfers between devices  82.3 us (23%)
  matrix products  40.4 us (11%)
  local copies, waits for them, and re-layouts  16.7 us (5%)
  starting transfers between devices  10.8 us (3%)
  other arithmetic  5.04 us (1%)
    all_to_all x1, blocking collectives, forward_transform(): lax.all_to_all(turned, 'ctx', split_axis=2, concat_axis=3, tiled=True)  108 us
    all_to_all x1, blocking collectives, inverse_transform(): lax.all_to_all(turned, 'ctx', split_axis=3, concat_axis=2, tiled=True)  63.1 us
    all_to_all x1, waiting for transfers between devices, forward_transform(): lax.all_to_all(stacked[:, None], 'ctx', split_axis=2, concat_axis=1, tile...  53.6 us
    all_to_all x1, blocking collectives, inverse_transform(): lax.all_to_all(blocks, 'ctx', split_axis=1, concat_axis=2, tiled=True)  34.2 us
    ppermute x4, waiting for transfers between devices, swapped(): return lax.ppermute(value, axis, pairs)  28.6 us
    all_to_all x1, starting transfers between devices, forward_transform(): lax.all_to_all(stacked[:, None], 'ctx', split_axis=2, concat_axis=1, tile...  7.57 us
  transfers between devices with their start and end apart: 5, of which 5 were waited for; matrix products, arithmetic and copies ran while one was open for 0% of the time, Pallas kernels for 0%

commit v1 on v0

v1 whole, which is shorter than its diff:
```python
import functools
import math

import jax
import jax.numpy as jnp
import ml_dtypes
import numpy as np
from jax import lax
from jax.experimental import pallas as pl
from jax.experimental.pallas import tpu as pltpu
from jax.sharding import PartitionSpec as P

MESH = pl.DeviceIdType.MESH


def plus(left, right):
    if left is None:
        return right
    return left if right is None else left + right


def minus(left, right):
    if right is None:
        return left
    return -right if left is None else left - right


def turn(value, cos, sin):
    real, imag = value
    if imag is None:
        return (real * cos, real * sin)
    return (real * cos - imag * sin, real * sin + imag * cos)


def real_forward(items):
    n = len(items)
    if n == 1:
        return [(items[0], None)]
    even, odd = real_forward(items[0::2]), real_forward(items[1::2])
    out = [None] * (n // 2 + 1)
    out[0] = (even[0][0] + odd[0][0], None)
    out[n // 2] = (even[0][0] - odd[0][0], None)
    for k in range(1, n // 4 + 1):
        if 4 * k == n:
            out[k] = (even[k][0], -odd[k][0])
            continue
        angle = -2.0 * math.pi * k / n
        turned = turn(odd[k], math.cos(angle), math.sin(angle))
        out[k] = (plus(even[k][0], turned[0]), plus(even[k][1], turned[1]))
        out[n // 2 - k] = (minus(even[k][0], turned[0]), minus(turned[1], even[k][1]))
    return out


def real_inverse(items, n):
    if n == 1:
        return [items[0][0]]
    first, last = items[0][0], items[n // 2][0]
    if n == 2:
        return [first + last, first - last]
    even, odd = [(first + last, None)], [(first - last, None)]
    for k in range(1, n // 4 + 1):
        real, imag = items[k]
        if 4 * k == n:
            even.append((2.0 * real, None))
            odd.append((-2.0 * imag, None))
            continue
        far_real, far_imag = items[n // 2 - k]
        angle = 2.0 * math.pi * k / n
        even.append((real + far_real, imag - far_imag))
        odd.append(turn((real - far_real, imag + far_imag), math.cos(angle), math.sin(angle)))
    out = [None] * n
    out[0::2] = real_inverse(even, n // 2)
    out[1::2] = real_inverse(odd, n // 2)
    return out


def split(value):
    high = value.astype(jnp.bfloat16)
    return high, (value - high.astype(jnp.float32)).astype(jnp.bfloat16)


def product(value, table_hi, table_lo):
    high, low = split(value)
    dot = functools.partial(jnp.dot, preferred_element_type=jnp.float32)
    return dot(high, table_hi) + (dot(low, table_hi) + dot(high, table_lo))


def kernel(
    n, nch, seqs, factor,
    x_ref, g_ref, f_ref, hi_ref, lo_ref, cos_ref, sin_ref,
    dx_ref, df_ref,
    send_f, send_d, recv_f, recv_d, back_send, back_recv,
    lhs, spec, eff, cross, mirror, flipped,
    fwd_send, fwd_recv, ret_send, ret_recv, pair_send, pair_recv,
):
    me = lax.axis_index("ctx")
    ch = lax.axis_index("ch")
    partner = nch - 1 - ch
    upper = (2 * ch) // nch
    width = x_ref.shape[1]
    rows = x_ref.shape[2] // n
    half = n // 2

    def chunk(owner):
        return owner + upper * (n - 1 - 2 * owner)

    def peer(step):
        return lax.rem(me + step, n)

    def to_filter(other):
        return pltpu.make_async_remote_copy(
            src_ref=send_f.at[chunk(other)], dst_ref=recv_f.at[me],
            send_sem=fwd_send.at[seqs, other], recv_sem=fwd_recv.at[seqs, me],
            device_id={"ctx": other}, device_id_type=MESH,
        )

    def from_filter(other):
        return pltpu.make_async_remote_copy(
            src_ref=send_f.at[chunk(other)], dst_ref=recv_f.at[other],
            send_sem=fwd_send.at[seqs, other], recv_sem=fwd_recv.at[seqs, other],
            device_id={"ctx": other}, device_id_type=MESH,
        )

    def to_data(b, other):
        return pltpu.make_async_remote_copy(
            src_ref=send_d.at[b, chunk(other)], dst_ref=recv_d.at[b, me],
            send_sem=fwd_send.at[b, other], recv_sem=fwd_recv.at[b, me],
            device_id={"ctx": other}, device_id_type=MESH,
        )

    def from_data(b, other):
        return pltpu.make_async_remote_copy(
            src_ref=send_d.at[b, chunk(other)], dst_ref=recv_d.at[b, other],
            send_sem=fwd_send.at[b, other], recv_sem=fwd_recv.at[b, other],
            device_id={"ctx": other}, device_id_type=MESH,
        )

    def to_back(b, other):
        return pltpu.make_async_remote_copy(
            src_ref=back_send.at[b, other], dst_ref=back_recv.at[b, chunk(me)],
            send_sem=ret_send.at[b, other], recv_sem=ret_recv.at[b, me],
            device_id={"ctx": other}, device_id_type=MESH,
        )

    def from_back(b, other):
        return pltpu.make_async_remote_copy(
            src_ref=back_send.at[b, other], dst_ref=back_recv.at[b, chunk(other)],
            send_sem=ret_send.at[b, other], recv_sem=ret_recv.at[b, other],
            device_id={"ctx": other}, device_id_type=MESH,
        )

    def to_pair(which, source):
        return pltpu.make_async_remote_copy(
            src_ref=source, dst_ref=mirror.at[which],
            send_sem=pair_send.at[which], recv_sem=pair_recv.at[which],
            device_id={"ch": partner}, device_id_type=MESH,
        )

    def each_peer(act):
        @pl.loop(1, n)
        def _(step):
            act(peer(step))

    def forward(arrays, count):
        for p, (real, imag) in enumerate(real_forward(arrays)):
            if p > 0:
                cos, sin = cos_ref[p : p + 1, :], sin_ref[p : p + 1, :]
                real, imag = turn((real, imag), cos, -sin)
            lhs[p, :count, :width] = real
            lhs[p, :count, width:] = jnp.zeros_like(real) if imag is None else imag
        flat = lhs[:, :count, :].reshape((half + 1) * count, 2 * width)
        out = product(flat, hi_ref[...], lo_ref[...])
        spec[:, :count, :] = out.reshape(half + 1, count, 2 * width)

    def inverse(b):
        flat = lhs[:, :rows, :].reshape((half + 1) * rows, 2 * width)
        out = product(flat, hi_ref[...], lo_ref[...])
        out = out.reshape(half + 1, rows, 2 * width) * factor
        items = []
        for p in range(half + 1):
            value = (out[p, :, :width], -out[p, :, width:])
            if p > 0:
                cos, sin = cos_ref[p : p + 1, :], sin_ref[p : p + 1, :]
                value = turn(value, cos, sin)
            items.append(value)
        for i, block in enumerate(real_inverse(items, n)):
            back_send[b, i] = block
        back_recv[b, chunk(me)] = back_send[b, me]
        each_peer(lambda other: to_back(b, other).start())

    def add_mirror(which, target):
        for r in range(rows):
            flipped[:, r : r + 1, :] = mirror[which, :, rows - 1 - r : rows - r, :]
        target[:, :, :width] += flipped[:, :, :width]
        target[:, :, width:] -= flipped[:, :, width:]

    barrier = pltpu.get_barrier_semaphore()
    each_peer(
        lambda other: pl.semaphore_signal(
            barrier, inc=1, device_id={"ctx": other}, device_id_type=MESH
        )
    )
    pl.semaphore_signal(barrier, inc=1, device_id={"ch": partner}, device_id_type=MESH)
    send_f[...] = f_ref[...].T.reshape(n, rows, width)
    pl.semaphore_wait(barrier, n)

    each_peer(lambda other: to_filter(other).start())
    recv_f[me] = send_f[chunk(me)]

    @pl.loop(0, seqs)
    def _(b):
        send_d[b, :, 0] = g_ref[b].T.reshape(n, rows, width)
        send_d[b, :, 1] = x_ref[b].T.reshape(n, rows, width)
        each_peer(lambda other: to_data(b, other).start())
        recv_d[b, me] = send_d[b, chunk(me)]

    each_peer(lambda other: from_filter(other).wait_recv())
    forward([recv_f[i] for i in range(n)], rows)
    eff[...] = spec[:, :rows, :]
    swap_f = to_pair(0, eff)
    swap_f.start()
    cross[...] = jnp.zeros_like(cross)
    swap_f.wait()
    add_mirror(0, eff)

    @pl.loop(0, seqs)
    def _(b):
        each_peer(lambda other: from_data(b, other).wait_recv())
        forward([recv_d[b, i].reshape(2 * rows, width) for i in range(n)], 2 * rows)
        g_re, g_im = spec[:, :rows, :width], spec[:, :rows, width:]
        x_re, x_im = spec[:, rows:, :width], spec[:, rows:, width:]
        cross[:, :, :width] += g_re * x_re + g_im * x_im
        cross[:, :, width:] += g_im * x_re - g_re * x_im
        e_re, e_im = eff[:, :, :width], eff[:, :, width:]
        lhs[:, :rows, :width] = e_re * g_re + e_im * g_im
        lhs[:, :rows, width:] = e_im * g_re - e_re * g_im
        inverse(b)

    swap_c = to_pair(1, cross)
    swap_c.start()
    swap_c.wait()
    add_mirror(1, cross)
    lhs[:, :rows, :width] = cross[:, :, :width]
    lhs[:, :rows, width:] = -cross[:, :, width:]
    inverse(seqs)

    @pl.loop(0, seqs)
    def _(b):
        each_peer(lambda other: from_back(b, other).wait_recv())
        dx_ref[b] = back_recv[b].reshape(n * rows, width).T

    each_peer(lambda other: from_back(seqs, other).wait_recv())
    df_ref[...] = back_recv[seqs].reshape(n * rows, width).T

    each_peer(lambda other: to_filter(other).wait_send())

    @pl.loop(0, seqs)
    def _(b):
        each_peer(lambda other: to_data(b, other).wait_send())

    @pl.loop(0, seqs + 1)
    def _(b):
        each_peer(lambda other: to_back(b, other).wait_send())


def tables(n, width):
    period = n * width
    turns = np.outer(np.arange(width), np.arange(width)) % width
    angle = turns * (2.0 * math.pi / width)
    cos, sin = np.cos(angle), np.sin(angle)
    table = np.block([[cos, -sin], [sin, cos]]).astype(np.float32)
    high = table.astype(ml_dtypes.bfloat16)
    low = (table - high.astype(np.float32)).astype(ml_dtypes.bfloat16)
    angle = np.outer(np.arange(n // 2 + 1), np.arange(width)) * (2.0 * math.pi / period)
    return high, low, np.cos(angle).astype(np.float32), np.sin(angle).astype(np.float32)


def body(n, nch, inputs, cotangent, filters):
    seqs, width, channels = inputs.shape
    rows = channels // n
    half = n // 2
    period = n * width
    factor = 1.0 / (period * math.sqrt(2.0 * period))
    high, low, cos, sin = (jnp.asarray(value) for value in tables(n, width))
    vmem = pl.BlockSpec(memory_space=pltpu.VMEM)
    real = jnp.float32
    dma = pltpu.SemaphoreType.DMA
    return tuple(pl.pallas_call(
        functools.partial(kernel, n, nch, seqs, factor),
        out_shape=(
            jax.ShapeDtypeStruct(inputs.shape, real),
            jax.ShapeDtypeStruct(filters.shape, real),
        ),
        in_specs=[vmem] * 7,
        out_specs=(vmem, vmem),
        scratch_shapes=[
            pltpu.VMEM((n, rows, width), real),
            pltpu.VMEM((seqs, n, 2, rows, width), real),
            pltpu.VMEM((n, rows, width), real),
            pltpu.VMEM((seqs, n, 2, rows, width), real),
            pltpu.VMEM((seqs + 1, n, rows, width), real),
            pltpu.VMEM((seqs + 1, n, rows, width), real),
            pltpu.VMEM((half + 1, 2 * rows, 2 * width), real),
            pltpu.VMEM((half + 1, 2 * rows, 2 * width), real),
            pltpu.VMEM((half + 1, rows, 2 * width), real),
            pltpu.VMEM((half + 1, rows, 2 * width), real),
            pltpu.VMEM((2, half + 1, rows, 2 * width), real),
            pltpu.VMEM((half + 1, rows, 2 * width), real),
            dma((seqs + 1, n)), dma((seqs + 1, n)),
            dma((seqs + 1, n)), dma((seqs + 1, n)),
            dma((2,)), dma((2,)),
        ],
        compiler_params=pltpu.CompilerParams(
            collective_id=0, has_side_effects=True, vmem_limit_bytes=56 * 2**20
        ),
    )(inputs, cotangent, filters, high, low, cos, sin))


def solution(mesh):
    in_specs = (P(None, "ctx", "ch"), P(None, "ctx", "ch"), P("ctx", "ch"))
    out_specs = (P(None, "ctx", "ch"), P("ctx", "ch"))
    run = functools.partial(body, mesh.shape["ctx"], mesh.shape["ch"])
    return jax.shard_map(run, mesh=mesh, in_specs=in_specs, out_specs=out_specs, check_vma=False)
```

time: 365 us -> 93.5 us (0.26)
  blocking collectives: 205 us -> 0 us
  Pallas kernels: 0 us -> 89.7 us
  waiting for transfers between devices: 82.3 us -> 0 us
  matrix products: 40.4 us -> 0 us
  local copies, waits for them, and re-layouts: 16.7 us -> 3.03 us
  starting transfers between devices: 10.8 us -> 0 us
  other arithmetic: 5.04 us -> 0 us
    all_to_all x3 -> x0, blocking collectives: 205 us -> none  [the longest x1 108 us: forward_transform(): lax.all_to_all(turned, 'ctx', split_axis=2, concat_axis=3, tiled=True)]
    pallas_call x0 -> x1, Pallas kernels: none -> 89.7 us  [body(): pl.pallas_call(functools.partial(kernel, n, nch, seqs, factor), out_shape...]
    all_to_all x1 -> x0, waiting for transfers between devices: 53.6 us -> none  [forward_transform(): lax.all_to_all(stacked[:, None], 'ctx', split_axis=2, concat_axis=1, tile...]
    dot_general x12 -> x0, matrix products: 40.4 us -> none  [the longest x1 5.12 us: forward_transform(): jnp.einsum('mj,kjc->kmc', sin_m, imag_in, precision=HIGHEST)]
    ppermute x4 -> x0, waiting for transfers between devices: 28.6 us -> none  [swapped(): return lax.ppermute(value, axis, pairs)]
    all_to_all x1 -> x0, starting transfers between devices: 7.57 us -> none  [forward_transform(): lax.all_to_all(stacked[:, None], 'ctx', split_axis=2, concat_axis=1, tile...]
    broadcast_in_dim x2 -> x0, local copies, waits for them, and re-layouts: 7.11 us -> none  [the longest x1 3.87 us: forward_transform(): stacked[:, None]]
    slice x4 -> x0, local copies, waits for them, and re-layouts: 4.51 us -> none  [the longest x1 2.02 us: inverse_transform(): gathered[1]]
  transfers between devices with their start and end apart: 5 -> 0, of which waited for: 5 -> 0; matrix products, arithmetic and copies ran while one was open for 0% -> 0% of each run, Pallas kernels for 0% -> 0%
where the time goes in v1:
time: 93.5 us; the launch traced here: 93.3 us
  Pallas kernels  89.7 us (96%)
  local copies, waits for them, and re-layouts  3.03 us (3%)
    pallas_call x1, Pallas kernels, body(): pl.pallas_call(functools.partial(kernel, n, nch, seqs, factor), out_shape...  89.7 us
    unnamed x4, local copies, waits for them, and re-layouts  3.03 us

profile of v1, /device:TPU:0, one launch (start us, length us, event | category | flops | bytes accessed | tf_op | source)
XLA Modules:
  0.0 93.3 jit_solution(16008596733802345984)
XLA Ops:
  0.6 89.7 %shard_map.86 = (f32[4,256,256]{2,1,0:T(8,128)}, f32[256,256]{1,0:T(8,128)}) custom-call(f32[4,256,256]{2,1,0:T(8,128)} %x_ref.1, f32[4,256,256]{2,1,0:T(8,128)} %g_ref.1, f32[256,256]{1,0:T(8,128)} %f_ref.1, bf16[512,512]{1,0:T(8,128)(2,1)} %constant.8.clone.hi_ref, bf16[512,512]{1,0:T(8,128)(2,1)} %constant.9.clone.lo_ref, ...), custom_call_target="tpu_custom_call" | custom-call | tf_op jit(solution)/shard_map/pallas_call | solution.py:288
  90.3 0.0 copy-start
  90.3 2.3 %copy.11 = f32[4,256,256]{2,1,0:T(8,128)} copy(f32[4,256,256]{2,1,0:T(8,128)} %get-tuple-element.4) | data formatting | bytes 2097152
  92.6 0.0 copy-done
  92.6 0.7 copy.12
Async XLA Ops:
  90.3 2.3 %copy-start = (f32[256,256]{1,0:T(8,128)S(1)}, f32[256,256]{1,0:T(8,128)}, u32[]{:S(2)}) copy-start(f32[256,256]{1,0:T(8,128)} %get-tuple-element.5) | copy-start | bytes 786436

commit v2 on v1

--- a/solution.py
+++ b/solution.py
@@ -87,11 +87,12 @@
 
 def kernel(
     n, nch, seqs, factor,
+    x_hbm, g_hbm, f_hbm, hi_hbm, lo_hbm, cos_hbm, sin_hbm,
+    dx_ref, df_ref,
     x_ref, g_ref, f_ref, hi_ref, lo_ref, cos_ref, sin_ref,
-    dx_ref, df_ref,
     send_f, send_d, recv_f, recv_d, back_send, back_recv,
     lhs, spec, eff, cross, mirror, flipped,
-    fwd_send, fwd_recv, ret_send, ret_recv, pair_send, pair_recv,
+    fwd_send, fwd_recv, ret_send, ret_recv, pair_send, pair_recv, load_sem, table_sem,
 ):
     me = lax.axis_index("ctx")
     ch = lax.axis_index("ch")
@@ -105,7 +106,18 @@
         return owner + upper * (n - 1 - 2 * owner)
 
     def peer(step):
-        return lax.rem(me + step, n)
+        mask = lax.rem(step + half - 2, n - 1) + 1
+        other = me
+        for bit in range(n.bit_length() - 1):
+            weight = 2**bit
+            other = other + lax.rem(mask // weight, 2) * weight * (1 - 2 * lax.rem(me // weight, 2))
+        return other
+
+    def load(b, which, source, target):
+        return pltpu.make_async_copy(source.at[b], target.at[b], load_sem.at[b, which])
+
+    def table(which, source, target):
+        return pltpu.make_async_copy(source, target, table_sem.at[which])
 
     def to_filter(other):
         return pltpu.make_async_remote_copy(
@@ -186,6 +198,8 @@
         for i, block in enumerate(real_inverse(items, n)):
             back_send[b, i] = block
         back_recv[b, chunk(me)] = back_send[b, me]
+
+    def give_back(b):
         each_peer(lambda other: to_back(b, other).start())
 
     def add_mirror(which, target):
@@ -194,6 +208,21 @@
         target[:, :, :width] += flipped[:, :, :width]
         target[:, :, width:] -= flipped[:, :, width:]
 
+    filter_load = table(0, f_hbm, f_ref)
+    filter_load.start()
+
+    @pl.loop(0, seqs)
+    def _(b):
+        load(b, 0, g_hbm, g_ref).start()
+        load(b, 1, x_hbm, x_ref).start()
+
+    table_loads = [
+        table(1, hi_hbm, hi_ref), table(2, lo_hbm, lo_ref),
+        table(3, cos_hbm, cos_ref), table(4, sin_hbm, sin_ref),
+    ]
+    for copy in table_loads:
+        copy.start()
+
     barrier = pltpu.get_barrier_semaphore()
     each_peer(
         lambda other: pl.semaphore_signal(
@@ -201,6 +230,7 @@
         )
     )
     pl.semaphore_signal(barrier, inc=1, device_id={"ch": partner}, device_id_type=MESH)
+    filter_load.wait()
     send_f[...] = f_ref[...].T.reshape(n, rows, width)
     pl.semaphore_wait(barrier, n)
 
@@ -209,11 +239,15 @@
 
     @pl.loop(0, seqs)
     def _(b):
+        load(b, 0, g_hbm, g_ref).wait()
+        load(b, 1, x_hbm, x_ref).wait()
         send_d[b, :, 0] = g_ref[b].T.reshape(n, rows, width)
         send_d[b, :, 1] = x_ref[b].T.reshape(n, rows, width)
         each_peer(lambda other: to_data(b, other).start())
         recv_d[b, me] = send_d[b, chunk(me)]
 
+    for copy in table_loads:
+        copy.wait()
     each_peer(lambda other: from_filter(other).wait_recv())
     forward([recv_f[i] for i in range(n)], rows)
     eff[...] = spec[:, :rows, :]
@@ -223,8 +257,7 @@
     swap_f.wait()
     add_mirror(0, eff)
 
-    @pl.loop(0, seqs)
-    def _(b):
+    def gradient(b):
         each_peer(lambda other: from_data(b, other).wait_recv())
         forward([recv_d[b, i].reshape(2 * rows, width) for i in range(n)], 2 * rows)
         g_re, g_im = spec[:, :rows, :width], spec[:, :rows, width:]
@@ -236,13 +269,24 @@
         lhs[:, :rows, width:] = e_im * g_re - e_re * g_im
         inverse(b)
 
+    pl.loop(0, seqs - 1)(gradient)
+    each_peer(lambda other: to_filter(other).wait_send())
+
+    @pl.loop(0, seqs)
+    def _(b):
+        each_peer(lambda other: to_data(b, other).wait_send())
+
+    pl.loop(0, seqs - 1)(give_back)
+    gradient(seqs - 1)
     swap_c = to_pair(1, cross)
     swap_c.start()
+    give_back(seqs - 1)
     swap_c.wait()
     add_mirror(1, cross)
     lhs[:, :rows, :width] = cross[:, :, :width]
     lhs[:, :rows, width:] = -cross[:, :, width:]
     inverse(seqs)
+    give_back(seqs)
 
     @pl.loop(0, seqs)
     def _(b):
@@ -251,12 +295,6 @@
 
     each_peer(lambda other: from_back(seqs, other).wait_recv())
     df_ref[...] = back_recv[seqs].reshape(n * rows, width).T
-
-    each_peer(lambda other: to_filter(other).wait_send())
-
-    @pl.loop(0, seqs)
-    def _(b):
-        each_peer(lambda other: to_data(b, other).wait_send())
 
     @pl.loop(0, seqs + 1)
     def _(b):
@@ -283,6 +321,7 @@
     factor = 1.0 / (period * math.sqrt(2.0 * period))
     high, low, cos, sin = (jnp.asarray(value) for value in tables(n, width))
     vmem = pl.BlockSpec(memory_space=pltpu.VMEM)
+    anywhere = pl.BlockSpec(memory_space=pl.ANY)
     real = jnp.float32
     dma = pltpu.SemaphoreType.DMA
     return tuple(pl.pallas_call(
@@ -291,9 +330,16 @@
             jax.ShapeDtypeStruct(inputs.shape, real),
             jax.ShapeDtypeStruct(filters.shape, real),
         ),
-        in_specs=[vmem] * 7,
+        in_specs=[anywhere] * 7,
         out_specs=(vmem, vmem),
         scratch_shapes=[
+            pltpu.VMEM(inputs.shape, real),
+            pltpu.VMEM(inputs.shape, real),
+            pltpu.VMEM(filters.shape, real),
+            pltpu.VMEM(high.shape, high.dtype),
+            pltpu.VMEM(low.shape, low.dtype),
+            pltpu.VMEM(cos.shape, real),
+            pltpu.VMEM(sin.shape, real),
             pltpu.VMEM((n, rows, width), real),
             pltpu.VMEM((seqs, n, 2, rows, width), real),
             pltpu.VMEM((n, rows, width), real),
@@ -308,7 +354,7 @@
             pltpu.VMEM((half + 1, rows, 2 * width), real),
             dma((seqs + 1, n)), dma((seqs + 1, n)),
             dma((seqs + 1, n)), dma((seqs + 1, n)),
-            dma((2,)), dma((2,)),
+            dma((2,)), dma((2,)), dma((seqs, 2)), dma((5,)),
         ],
         compiler_params=pltpu.CompilerParams(
             collective_id=0, has_side_effects=True, vmem_limit_bytes=56 * 2**20

time: 93.5 us -> 93.5 us (level)
  no operation moved by 1% of the time
where the time goes in v2:
time: 93.5 us; the launch traced here: 93.4 us
  Pallas kernels  89.7 us (96%)
  local copies, waits for them, and re-layouts  3.03 us (3%)
    pallas_call x1, Pallas kernels, body(): pl.pallas_call(functools.partial(kernel, n, nch, seqs, factor), out_shape...  89.7 us
    unnamed x4, local copies, waits for them, and re-layouts  3.03 us

profile of v2, /device:TPU:0, one launch (start us, length us, event | category | flops | bytes accessed | tf_op | source)
XLA Modules:
  0.0 93.4 jit_solution(15681270680041131768)
XLA Ops:
  0.6 89.7 %shard_map.86 = (f32[4,256,256]{2,1,0:T(8,128)}, f32[256,256]{1,0:T(8,128)}) custom-call(f32[4,256,256]{2,1,0:T(8,128)} %x_hbm.1, f32[4,256,256]{2,1,0:T(8,128)} %g_hbm.1, f32[256,256]{1,0:T(8,128)} %f_hbm.1, bf16[512,512]{1,0:T(8,128)(2,1)} %constant.8.clone.hi_hbm, bf16[512,512]{1,0:T(8,128)(2,1)} %constant.9.clone.lo_hbm, ...), custom_call_target="tpu_custom_call" | custom-call | tf_op jit(solution)/shard_map/pallas_call | solution.py:327
  90.3 0.0 copy-start
  90.3 2.3 %copy.11 = f32[4,256,256]{2,1,0:T(8,128)} copy(f32[4,256,256]{2,1,0:T(8,128)} %get-tuple-element.4) | data formatting | bytes 2097152
  92.7 0.0 copy-done
  92.7 0.7 copy.12
Async XLA Ops:
  90.3 2.3 %copy-start = (f32[256,256]{1,0:T(8,128)S(1)}, f32[256,256]{1,0:T(8,128)}, u32[]{:S(2)}) copy-start(f32[256,256]{1,0:T(8,128)} %get-tuple-element.5) | copy-start | bytes 786436

commit v3 on v2

--- a/solution.py
+++ b/solution.py
@@ -327,8 +327,8 @@
     return tuple(pl.pallas_call(
         functools.partial(kernel, n, nch, seqs, factor),
         out_shape=(
-            jax.ShapeDtypeStruct(inputs.shape, real),
-            jax.ShapeDtypeStruct(filters.shape, real),
+            pltpu.VMEM(inputs.shape, real),
+            pltpu.VMEM(filters.shape, real),
         ),
         in_specs=[anywhere] * 7,
         out_specs=(vmem, vmem),

time: 93.5 us -> 91.1 us (0.974)
  local copies, waits for them, and re-layouts: 3.03 us -> 1.67 us
  Pallas kernels: 89.7 us -> 88.6 us
    unnamed x4 -> x2, local copies, waits for them, and re-layouts: 3.03 us -> 1.67 us
    pallas_call x1, Pallas kernels: 89.7 us -> 88.6 us  [body(): pl.pallas_call(functools.partial(kernel, n, nch, seqs, factor), out_shape...]
where the time goes in v3:
time: 91.1 us; the launch traced here: 90.9 us
  Pallas kernels  88.6 us (97%)
  local copies, waits for them, and re-layouts  1.67 us (2%)
    pallas_call x1, Pallas kernels, body(): pl.pallas_call(functools.partial(kernel, n, nch, seqs, factor), out_shape...  88.6 us

profile of v3, /device:TPU:0, one launch (start us, length us, event | category | flops | bytes accessed | tf_op | source)
XLA Modules:
  0.0 90.9 jit_solution(15086310857149326659)
XLA Ops:
  0.6 88.6 %shard_map.86 = (f32[4,256,256]{2,1,0:T(8,128)S(1)}, f32[256,256]{1,0:T(8,128)S(1)}) custom-call(f32[4,256,256]{2,1,0:T(8,128)} %x_hbm.1, f32[4,256,256]{2,1,0:T(8,128)} %g_hbm.1, f32[256,256]{1,0:T(8,128)} %f_hbm.1, bf16[512,512]{1,0:T(8,128)(2,1)} %constant.8.clone.hi_hbm, bf16[512,512]{1,0:T(8,128)(2,1)} %constant.9.clone.lo_hbm, ...), custom_call_target="tpu_custom_call" | custom-call | tf_op jit(solution)/shard_map/pallas_call | solution.py:327
  89.3 1.0 %copy.11 = f32[4,256,256]{2,1,0:T(8,128)} copy(f32[4,256,256]{2,1,0:T(8,128)S(1)} %get-tuple-element.2) | data formatting | bytes 2097152
  90.2 0.7 copy.12

commit v4 on v3

--- a/solution.py
+++ b/solution.py
@@ -211,6 +211,14 @@
     filter_load = table(0, f_hbm, f_ref)
     filter_load.start()
 
+    barrier = pltpu.get_barrier_semaphore()
+    each_peer(
+        lambda other: pl.semaphore_signal(
+            barrier, inc=1, device_id={"ctx": other}, device_id_type=MESH
+        )
+    )
+    pl.semaphore_signal(barrier, inc=1, device_id={"ch": partner}, device_id_type=MESH)
+
     @pl.loop(0, seqs)
     def _(b):
         load(b, 0, g_hbm, g_ref).start()
@@ -223,13 +231,6 @@
     for copy in table_loads:
         copy.start()
 
-    barrier = pltpu.get_barrier_semaphore()
-    each_peer(
-        lambda other: pl.semaphore_signal(
-            barrier, inc=1, device_id={"ctx": other}, device_id_type=MESH
-        )
-    )
-    pl.semaphore_signal(barrier, inc=1, device_id={"ch": partner}, device_id_type=MESH)
     filter_load.wait()
     send_f[...] = f_ref[...].T.reshape(n, rows, width)
     pl.semaphore_wait(barrier, n)
@@ -301,6 +302,17 @@
         each_peer(lambda other: to_back(b, other).wait_send())
 
 
+def write_out(dx_ref, df_ref, dx_hbm, df_hbm, sems):
+    copies = [
+        pltpu.make_async_copy(dx_ref, dx_hbm, sems.at[0]),
+        pltpu.make_async_copy(df_ref, df_hbm, sems.at[1]),
+    ]
+    for copy in copies:
+        copy.start()
+    for copy in copies:
+        copy.wait()
+
+
 def tables(n, width):
     period = n * width
     turns = np.outer(np.arange(width), np.arange(width)) % width
@@ -324,7 +336,7 @@
     anywhere = pl.BlockSpec(memory_space=pl.ANY)
     real = jnp.float32
     dma = pltpu.SemaphoreType.DMA
-    return tuple(pl.pallas_call(
+    grads = pl.pallas_call(
         functools.partial(kernel, n, nch, seqs, factor),
         out_shape=(
             pltpu.VMEM(inputs.shape, real),
@@ -359,7 +371,17 @@
         compiler_params=pltpu.CompilerParams(
             collective_id=0, has_side_effects=True, vmem_limit_bytes=56 * 2**20
         ),
-    )(inputs, cotangent, filters, high, low, cos, sin))
+    )(inputs, cotangent, filters, high, low, cos, sin)
+    return tuple(pl.pallas_call(
+        write_out,
+        out_shape=(
+            jax.ShapeDtypeStruct(inputs.shape, real),
+            jax.ShapeDtypeStruct(filters.shape, real),
+        ),
+        in_specs=[vmem, vmem],
+        out_specs=(anywhere, anywhere),
+        scratch_shapes=[dma((2,))],
+    )(*grads))
 
 
 def solution(mesh):

time: 91.1 us -> 93.4 us (1.025)
  Pallas kernels: 88.6 us -> 90.9 us
    pallas_call x0 -> x1, Pallas kernels: none -> 2.33 us  [body(): pl.pallas_call(write_out, out_shape=(jax.ShapeDtypeStruct(inputs.shape, r...]
where the time goes in v4:
time: 93.4 us; the launch traced here: 93.2 us
  Pallas kernels  90.9 us (97%)
  local copies, waits for them, and re-layouts  1.67 us (2%)
    pallas_call x1, Pallas kernels, body(): pl.pallas_call(functools.partial(kernel, n, nch, seqs, factor), out_shape...  88.6 us
    pallas_call x1, Pallas kernels, body(): pl.pallas_call(write_out, out_shape=(jax.ShapeDtypeStruct(inputs.shape, r...  2.33 us

profile of v4, /device:TPU:0, one launch (start us, length us, event | category | flops | bytes accessed | tf_op | source)
XLA Modules:
  0.0 93.2 jit_solution(12211514426947203744)
XLA Ops:
  0.6 88.6 %shard_map.86 = (f32[4,256,256]{2,1,0:T(8,128)S(1)}, f32[256,256]{1,0:T(8,128)S(1)}) custom-call(f32[4,256,256]{2,1,0:T(8,128)} %x_hbm.1, f32[4,256,256]{2,1,0:T(8,128)} %g_hbm.1, f32[256,256]{1,0:T(8,128)} %f_hbm.1, bf16[512,512]{1,0:T(8,128)(2,1)} %constant.8.clone.hi_hbm, bf16[512,512]{1,0:T(8,128)(2,1)} %constant.9.clone.lo_hbm, ...), custom_call_target="tpu_custom_call" | custom-call | tf_op jit(solution)/shard_map/pallas_call | solution.py:339
  89.2 0.0 copy-start
  89.2 1.0 %copy-done = f32[4,256,256]{2,1,0:T(8,128)} copy-done((f32[4,256,256]{2,1,0:T(8,128)}, f32[4,256,256]{2,1,0:T(8,128)S(1)}, u32[]{:S(2)}) %copy-start) | copy-done | bytes 1048600
  90.2 0.0 copy-start.1
  90.2 0.7 copy-done.1
  90.9 2.3 %shard_map.87 = (f32[4,256,256]{2,1,0:T(8,128)}, f32[256,256]{1,0:T(8,128)}) custom-call(f32[4,256,256]{2,1,0:T(8,128)} %copy-done, f32[256,256]{1,0:T(8,128)} %copy-done.1), custom_call_target="tpu_custom_call" | custom-call | tf_op jit(solution)/shard_map/pallas_call | solution.py:375
Async XLA Ops:
  89.2 1.0 %copy-start = (f32[4,256,256]{2,1,0:T(8,128)}, f32[4,256,256]{2,1,0:T(8,128)S(1)}, u32[]{:S(2)}) copy-start(f32[4,256,256]{2,1,0:T(8,128)S(1)} %get-tuple-element.4.dx_ref) | copy-start | bytes 3145732
  90.2 0.7 copy-start.1

commit v5 on v4

--- a/solution.py
+++ b/solution.py
@@ -271,13 +271,14 @@
         inverse(b)
 
     pl.loop(0, seqs - 1)(gradient)
+    give_back(0)
     each_peer(lambda other: to_filter(other).wait_send())
 
     @pl.loop(0, seqs)
     def _(b):
         each_peer(lambda other: to_data(b, other).wait_send())
 
-    pl.loop(0, seqs - 1)(give_back)
+    pl.loop(1, seqs - 1)(give_back)
     gradient(seqs - 1)
     swap_c = to_pair(1, cross)
     swap_c.start()
@@ -381,6 +382,7 @@
         in_specs=[vmem, vmem],
         out_specs=(anywhere, anywhere),
         scratch_shapes=[dma((2,))],
+        compiler_params=pltpu.CompilerParams(vmem_limit_bytes=2**20),
     )(*grads))
 
 

time: 93.4 us -> 90.3 us (0.967)
  local copies, waits for them, and re-layouts: 1.67 us -> 0 us
  Pallas kernels: 90.9 us -> 89.5 us
    unnamed x4 -> x0, local copies, waits for them, and re-layouts: 1.67 us -> none
    pallas_call x1, Pallas kernels: 2.33 us -> 1.07 us  [body(): pl.pallas_call(write_out, out_shape=(jax.ShapeDtypeStruct(inputs.shape, r...]
where the time goes in v5:
time: 90.3 us; the launch traced here: 90.1 us
  Pallas kernels  89.5 us (99%)
    pallas_call x1, Pallas kernels, body(): pl.pallas_call(functools.partial(kernel, n, nch, seqs, factor), out_shape...  88.4 us

profile of v5, /device:TPU:0, one launch (start us, length us, event | category | flops | bytes accessed | tf_op | source)
XLA Modules:
  0.0 90.1 jit_solution(14483418024701699328)
XLA Ops:
  0.6 88.4 %shard_map.86 = (f32[4,256,256]{2,1,0:T(8,128)S(1)}, f32[256,256]{1,0:T(8,128)S(1)}) custom-call(f32[4,256,256]{2,1,0:T(8,128)} %x_hbm.1, f32[4,256,256]{2,1,0:T(8,128)} %g_hbm.1, f32[256,256]{1,0:T(8,128)} %f_hbm.1, bf16[512,512]{1,0:T(8,128)(2,1)} %constant.8.clone.hi_hbm, bf16[512,512]{1,0:T(8,128)(2,1)} %constant.9.clone.lo_hbm, ...), custom_call_target="tpu_custom_call" | custom-call | tf_op jit(solution)/shard_map/pallas_call | solution.py:340
  89.1 1.1 %shard_map.87 = (f32[4,256,256]{2,1,0:T(8,128)}, f32[256,256]{1,0:T(8,128)}) custom-call(f32[4,256,256]{2,1,0:T(8,128)S(1)} %get-tuple-element.4.dx_ref, f32[256,256]{1,0:T(8,128)S(1)} %get-tuple-element.5.df_ref), custom_call_target="tpu_custom_call" | custom-call | tf_op jit(solution)/shard_map/pallas_call | solution.py:376

commit v6 on v5

--- a/solution.py
+++ b/solution.py
@@ -106,7 +106,7 @@
         return owner + upper * (n - 1 - 2 * owner)
 
     def peer(step):
-        mask = lax.rem(step + half - 2, n - 1) + 1
+        mask = step // 2 + lax.rem(step, 2) * half
         other = me
         for bit in range(n.bit_length() - 1):
             weight = 2**bit

time: 90.3 us -> 90.1 us (level)
  no operation moved by 1% of the time
where the time goes in v6:
time: 90.1 us; the launch traced here: 89.9 us
  Pallas kernels  89.3 us (99%)
    pallas_call x1, Pallas kernels, body(): pl.pallas_call(functools.partial(kernel, n, nch, seqs, factor), out_shape...  88.2 us

profile of v6, /device:TPU:0, one launch (start us, length us, event | category | flops | bytes accessed | tf_op | source)
XLA Modules:
  0.0 89.9 jit_solution(10954370797400306422)
XLA Ops:
  0.6 88.2 %shard_map.86 = (f32[4,256,256]{2,1,0:T(8,128)S(1)}, f32[256,256]{1,0:T(8,128)S(1)}) custom-call(f32[4,256,256]{2,1,0:T(8,128)} %x_hbm.1, f32[4,256,256]{2,1,0:T(8,128)} %g_hbm.1, f32[256,256]{1,0:T(8,128)} %f_hbm.1, bf16[512,512]{1,0:T(8,128)(2,1)} %constant.8.clone.hi_hbm, bf16[512,512]{1,0:T(8,128)(2,1)} %constant.9.clone.lo_hbm, ...), custom_call_target="tpu_custom_call" | custom-call | tf_op jit(solution)/shard_map/pallas_call | solution.py:340
  88.9 1.1 %shard_map.87 = (f32[4,256,256]{2,1,0:T(8,128)}, f32[256,256]{1,0:T(8,128)}) custom-call(f32[4,256,256]{2,1,0:T(8,128)S(1)} %get-tuple-element.4.dx_ref, f32[256,256]{1,0:T(8,128)S(1)} %get-tuple-element.5.df_ref), custom_call_target="tpu_custom_call" | custom-call | tf_op jit(solution)/shard_map/pallas_call | solution.py:376

commit v7 on v6

--- a/solution.py
+++ b/solution.py
@@ -270,15 +270,11 @@
         lhs[:, :rows, width:] = e_im * g_re - e_re * g_im
         inverse(b)
 
-    pl.loop(0, seqs - 1)(gradient)
-    give_back(0)
-    each_peer(lambda other: to_filter(other).wait_send())
-
-    @pl.loop(0, seqs)
-    def _(b):
-        each_peer(lambda other: to_data(b, other).wait_send())
-
-    pl.loop(1, seqs - 1)(give_back)
+    @pl.loop(0, seqs - 1)
+    def _(b):
+        gradient(b)
+        give_back(b)
+
     gradient(seqs - 1)
     swap_c = to_pair(1, cross)
     swap_c.start()
@@ -297,6 +293,12 @@
 
     each_peer(lambda other: from_back(seqs, other).wait_recv())
     df_ref[...] = back_recv[seqs].reshape(n * rows, width).T
+
+    each_peer(lambda other: to_filter(other).wait_send())
+
+    @pl.loop(0, seqs)
+    def _(b):
+        each_peer(lambda other: to_data(b, other).wait_send())
 
     @pl.loop(0, seqs + 1)
     def _(b):

time: 90.1 us -> 91.1 us (1.011)
  Pallas kernels: 89.3 us -> 90.3 us
    pallas_call x1, Pallas kernels: 88.2 us -> 89.2 us  [body(): pl.pallas_call(functools.partial(kernel, n, nch, seqs, factor), out_shape...]
where the time goes in v7:
time: 91.1 us; the launch traced here: 90.9 us
  Pallas kernels  90.3 us (99%)
    pallas_call x1, Pallas kernels, body(): pl.pallas_call(functools.partial(kernel, n, nch, seqs, factor), out_shape...  89.2 us

profile of v7, /device:TPU:0, one launch (start us, length us, event | category | flops | bytes accessed | tf_op | source)
XLA Modules:
  0.0 90.9 jit_solution(11051599958855545495)
XLA Ops:
  0.6 89.2 %shard_map.86 = (f32[4,256,256]{2,1,0:T(8,128)S(1)}, f32[256,256]{1,0:T(8,128)S(1)}) custom-call(f32[4,256,256]{2,1,0:T(8,128)} %x_hbm.1, f32[4,256,256]{2,1,0:T(8,128)} %g_hbm.1, f32[256,256]{1,0:T(8,128)} %f_hbm.1, bf16[512,512]{1,0:T(8,128)(2,1)} %constant.8.clone.hi_hbm, bf16[512,512]{1,0:T(8,128)(2,1)} %constant.9.clone.lo_hbm, ...), custom_call_target="tpu_custom_call" | custom-call | tf_op jit(solution)/shard_map/pallas_call | solution.py:342
  89.8 1.1 %shard_map.87 = (f32[4,256,256]{2,1,0:T(8,128)}, f32[256,256]{1,0:T(8,128)}) custom-call(f32[4,256,256]{2,1,0:T(8,128)S(1)} %get-tuple-element.4.dx_ref, f32[256,256]{1,0:T(8,128)S(1)} %get-tuple-element.5.df_ref), custom_call_target="tpu_custom_call" | custom-call | tf_op jit(solution)/shard_map/pallas_call | solution.py:378

commit v8 on v6

--- a/solution.py
+++ b/solution.py
@@ -238,14 +238,17 @@
     each_peer(lambda other: to_filter(other).start())
     recv_f[me] = send_f[chunk(me)]
 
-    @pl.loop(0, seqs)
-    def _(b):
+    first = min(2, seqs)
+
+    def prepare(b):
         load(b, 0, g_hbm, g_ref).wait()
         load(b, 1, x_hbm, x_ref).wait()
         send_d[b, :, 0] = g_ref[b].T.reshape(n, rows, width)
         send_d[b, :, 1] = x_ref[b].T.reshape(n, rows, width)
         each_peer(lambda other: to_data(b, other).start())
         recv_d[b, me] = send_d[b, chunk(me)]
+
+    pl.loop(0, first)(prepare)
 
     for copy in table_loads:
         copy.wait()
@@ -270,11 +273,17 @@
         lhs[:, :rows, width:] = e_im * g_re - e_re * g_im
         inverse(b)
 
-    pl.loop(0, seqs - 1)(gradient)
+    @pl.loop(0, seqs - first)
+    def _(b):
+        each_peer(lambda other: to_data(b, other).wait_send())
+        prepare(b + first)
+        gradient(b)
+
+    pl.loop(seqs - first, seqs - 1)(gradient)
     give_back(0)
     each_peer(lambda other: to_filter(other).wait_send())
 
-    @pl.loop(0, seqs)
+    @pl.loop(seqs - first, seqs)
     def _(b):
         each_peer(lambda other: to_data(b, other).wait_send())
 

time: 90.1 us -> 90.1 us (level)
  no operation moved by 1% of the time
where the time goes in v8:
time: 90.1 us; the launch traced here: 90 us
  Pallas kernels  89.3 us (99%)
    pallas_call x1, Pallas kernels, body(): pl.pallas_call(functools.partial(kernel, n, nch, seqs, factor), out_shape...  88.3 us

profile of v8, /device:TPU:0, one launch (start us, length us, event | category | flops | bytes accessed | tf_op | source)
XLA Modules:
  0.0 90.0 jit_solution(17216284130519830646)
XLA Ops:
  0.6 88.3 %shard_map.86 = (f32[4,256,256]{2,1,0:T(8,128)S(1)}, f32[256,256]{1,0:T(8,128)S(1)}) custom-call(f32[4,256,256]{2,1,0:T(8,128)} %x_hbm.1, f32[4,256,256]{2,1,0:T(8,128)} %g_hbm.1, f32[256,256]{1,0:T(8,128)} %f_hbm.1, bf16[512,512]{1,0:T(8,128)(2,1)} %constant.8.clone.hi_hbm, bf16[512,512]{1,0:T(8,128)(2,1)} %constant.9.clone.lo_hbm, ...), custom_call_target="tpu_custom_call" | custom-call | tf_op jit(solution)/shard_map/pallas_call | solution.py:349
  88.9 1.1 %shard_map.87 = (f32[4,256,256]{2,1,0:T(8,128)}, f32[256,256]{1,0:T(8,128)}) custom-call(f32[4,256,256]{2,1,0:T(8,128)S(1)} %get-tuple-element.4.dx_ref, f32[256,256]{1,0:T(8,128)S(1)} %get-tuple-element.5.df_ref), custom_call_target="tpu_custom_call" | custom-call | tf_op jit(solution)/shard_map/pallas_call | solution.py:385
